TPU v7x, 32 devices: a whole 2x2x4 slice. The times are simulated.
32 devices in a mesh: batch: 4 (over y, x), tok: 8 (over z, core).
Axes of the slice: x: 2, y: 2, z: 4, core: 2. Of those that a mesh axis runs over, the one named last changes fastest.
Arguments:
- inner_first: bfloat16 [512, 2048], P(('batch', 'tok')), parts along dimension 0, may hold values from -6 to 6
- gate_first: bfloat16 [512, 2048], P(('batch', 'tok')), parts along dimension 0, may hold values from -6 to 6
- bc_first: bfloat16 [512, 256], P(('batch', 'tok')), parts along dimension 0, may hold values from -4 to 4
- first_raw_steps: float32 [512, 32], P(('batch', 'tok')), parts along dimension 0
- rate_first: float32 [32], replicated, may hold values from 0 to 4
- bias_first: float32 [32], replicated, may hold values from -9 to -2.5
- skip_first: float32 [32], replicated, may hold values from 0.5 to 1.5
- norm_gain: float32 [2048], replicated, may hold values from 0.25 to 1.75
- out_weight: bfloat16 [2048, 2048], P('tok'), may hold values from -0.125 to 0.125
- residual: bfloat16 [512, 2048], P(('batch', 'tok')), parts along dimension 0, may hold values from -6 to 6
- pre_gain: float32 [2048], replicated, may hold values from 0.25 to 1.75
- in_weight: bfloat16 [2048, 2304], P('tok'), may hold values from -0.125 to 0.125
- conv_weight: bfloat16 [4, 2304], replicated, may hold values from -3 to 3
- conv_bias: float32 [2304], replicated, may hold values from -3 to 3
- step_weight: bfloat16 [2048, 32], replicated, may hold values from -0.0625 to 0.0625
- bias_second: float32 [32], replicated, may hold values from -9 to -2.5
- rate_second: float32 [32], replicated, may hold values from 0 to 4
- skip_second: float32 [32], replicated, may hold values from 0.5 to 1.5
- final_gain: float32 [2048], replicated, may hold values from 0.25 to 1.75
Outputs:
- mixed: bfloat16 [512, 2048], P(('batch', 'tok')), parts along dimension 0
There are 4 independent parts, one for each index of `batch`. A program takes and returns all parts, laid end to end along the dimension named above; an argument that names none is the same for every part. Nothing has to cross between parts.
All inputs are finite; a program needn't handle non-finite values.
Results may differ from a plain program's by a relative error of at most 0.0075.
Values may be sent and summed in bfloat16 or wider, within the bound.
A program may use at most 192 MiB of HBM per device.

v0:
```python
import jax
import jax.numpy as jnp
from jax import lax
from jax.sharding import PartitionSpec as P

KC = 4
COL_DEV = 1


def prefix(value, axis, combine, identity):
    peers, here = (lax.axis_size(axis), lax.axis_index(axis))
    everything = jax.tree.map(lambda part: lax.all_gather(part, axis), value)
    start = jax.tree.map(
        lambda part, zero: jnp.broadcast_to(jnp.asarray(zero, part.dtype), part.shape),
        value,
        identity,
    )

    def hop(k, before):
        reached = k < here
        new = combine(before, jax.tree.map(lambda part: part[k], everything))
        return jax.tree.map(lambda a, b: jnp.where(reached, a, b), new, before)

    return lax.fori_loop(0, peers, hop, start)


def shifted(value, axis, steps):
    count = lax.axis_size(axis)
    first, last = (max(0, -steps), min(count, count - steps))
    return lax.ppermute(value, axis, [(source, source + steps) for source in range(first, last)])


def chain_join(earlier, following):
    early_decay, early_state = earlier
    late_decay, late_state = following
    return (early_decay + late_decay, jnp.exp(late_decay)[:, None, None] * early_state + late_state)


def advance(entering, scan_item):
    block_decay, block_state = scan_item
    return (jnp.exp(block_decay)[:, None, None] * entering + block_state, entering)


def rms_scale(matrix, gains):
    return (
        matrix
        * lax.rsqrt(jnp.mean(matrix * matrix, axis=-1, keepdims=True) + 1e-05)
        * gains[None, :]
    )


def entering_state(device_decay, local_final):
    heads, state_width, head_width = local_final.shape
    zero_state = jnp.zeros((heads, state_width, head_width), jnp.float32)
    ignored, incoming = prefix(
        (device_decay, local_final),
        "tok",
        chain_join,
        (jnp.zeros((heads,), jnp.float32), zero_state),
    )
    return incoming


def ssd_local(values, write_side, read_side, steps, rates, skips):
    tok_rows = values.shape[0]
    heads = rates.shape[0]
    head_width = values.shape[1] // heads
    state_width = write_side.shape[1]
    block_len = min(256, tok_rows)
    blocks = tok_rows // block_len
    step_blocks = steps.reshape(blocks, block_len, heads)
    cumulative = jnp.cumsum(-rates[None, None, :] * step_blocks, axis=1)
    value_blocks = values.reshape(blocks, block_len, heads, head_width)
    write_blocks = write_side.reshape(blocks, block_len, state_width)
    read_blocks = read_side.reshape(blocks, block_len, state_width)
    write_scale = jnp.exp(cumulative[:, -1:, :] - cumulative) * step_blocks
    written = (write_blocks[:, :, None, :].astype(jnp.float32) * write_scale[:, :, :, None]).astype(
        jnp.bfloat16
    )
    block_states = jnp.einsum(
        "bqhn,bqhp->bhnp", written, value_blocks, preferred_element_type=jnp.float32
    )
    block_decay = cumulative[:, -1, :]
    zero_state = jnp.zeros((heads, state_width, head_width), jnp.float32)
    local_final, local_entry = lax.scan(advance, zero_state, (block_decay, block_states))
    device_decay = jnp.sum(block_decay, axis=0)
    incoming = entering_state(device_decay, local_final)
    decay_before = jnp.cumsum(block_decay, axis=0) - block_decay
    entry = local_entry + jnp.exp(decay_before)[:, :, None, None] * incoming[None]
    intersections = jnp.einsum(
        "btn,bsn->bts", read_blocks, write_blocks, preferred_element_type=jnp.float32
    )
    by_head = jnp.transpose(cumulative, (0, 2, 1))
    lower_mask = jnp.tril(jnp.ones((block_len, block_len), bool))
    decay = jnp.exp(
        jnp.where(lower_mask[None, None], by_head[:, :, :, None] - by_head[:, :, None, :], -jnp.inf)
    )
    step_heads = jnp.transpose(step_blocks, (0, 2, 1))
    mixing = (intersections[:, None] * decay * step_heads[:, :, None, :]).astype(jnp.bfloat16)
    diagonal = jnp.einsum(
        "bhts,bshp->bthp", mixing, value_blocks, preferred_element_type=jnp.float32
    )
    carried = (
        jnp.einsum(
            "btn,bhnp->bthp",
            read_blocks.astype(jnp.float32),
            entry,
            precision=lax.Precision.HIGHEST,
        )
        * jnp.exp(cumulative)[:, :, :, None]
    )
    result = diagonal + carried + skips[None, None, :, None] * value_blocks.astype(jnp.float32)
    return result.reshape(tok_rows, heads * head_width)


def local(
    inner_first,
    gate_first,
    bc_first,
    first_raw_steps,
    rate_first,
    bias_first,
    skip_first,
    norm_gain,
    out_weight,
    residual,
    pre_gain,
    in_weight,
    conv_weight,
    conv_bias,
    step_weight,
    bias_second,
    rate_second,
    skip_second,
    final_gain,
):
    state_width = bc_first.shape[1] // 2
    inner_width = inner_first.shape[1]
    model_width = residual.shape[1]
    out_whole, in_whole = (
        lax.all_gather(out_weight, "tok", axis=0, tiled=True),
        lax.all_gather(in_weight, "tok", axis=0, tiled=True),
    )
    steps_one = jax.nn.softplus(first_raw_steps + bias_first[None, :])
    scanned_one = ssd_local(
        inner_first,
        bc_first[:, :state_width],
        bc_first[:, state_width:],
        steps_one,
        rate_first,
        skip_first,
    )
    gated = scanned_one * jax.nn.silu(gate_first.astype(jnp.float32))
    normed_one = rms_scale(gated, norm_gain).astype(jnp.bfloat16)
    hidden_raster = (
        residual.astype(jnp.float32)
        + jnp.dot(normed_one, out_whole, preferred_element_type=jnp.float32)
    ).astype(jnp.bfloat16)
    tok_rows = hidden_raster.shape[0]
    peers = lax.axis_size("tok")
    raster_rows = tok_rows // (peers * COL_DEV)
    outgoing = hidden_raster.reshape(raster_rows, peers, COL_DEV, model_width).transpose(2, 1, 0, 3)
    arrived = lax.all_to_all(outgoing, "tok", split_axis=1, concat_axis=1, tiled=True)
    hidden_column = arrived.reshape(tok_rows, model_width)
    pre_normed = rms_scale(hidden_column.astype(jnp.float32), pre_gain).astype(jnp.bfloat16)
    rim_width = KC - 1
    projected = jnp.dot(pre_normed, in_whole, preferred_element_type=jnp.float32).astype(
        jnp.bfloat16
    )
    rim_projected = shifted(projected[tok_rows - rim_width :], "tok", 1)
    padded = jnp.concatenate([rim_projected, projected], axis=0)
    summed = conv_bias[None, :]
    for offset in range(KC):
        summed = (
            summed
            + conv_weight[offset].astype(jnp.float32)[None, :] * padded[offset : offset + tok_rows]
        )
    convolved = jax.nn.silu(summed).astype(jnp.bfloat16)
    steps_two = jax.nn.softplus(
        jnp.dot(pre_normed, step_weight, preferred_element_type=jnp.float32) + bias_second[None, :]
    )
    scanned_two = ssd_local(
        convolved[:, :inner_width],
        convolved[:, inner_width : inner_width + state_width],
        convolved[:, inner_width + state_width :],
        steps_two,
        rate_second,
        skip_second,
    )
    return rms_scale(scanned_two, final_gain).astype(jnp.bfloat16)


def solution(mesh):
    placed = (
        P(("batch", "tok"), None),
        P(("batch", "tok"), None),
        P(("batch", "tok"), None),
        P(("batch", "tok"), None),
        P(),
        P(),
        P(),
        P(),
        P("tok", None),
        P(("batch", "tok"), None),
        P(),
        P("tok", None),
        P(),
        P(),
        P(),
        P(),
        P(),
        P(),
        P(),
    )
    return jax.shard_map(
        local, mesh=mesh, in_specs=placed, out_specs=P(("batch", "tok"), None), check_vma=False
    )
```

profile of v0, /device:TPU:0, one launch (start us, length us, event | category | flops | bytes accessed | tf_op | source)
XLA Modules:
  0.0 414.8 jit_solution(10963695424799935862)
XLA Ops:
  14.7 13.4 %all-gather = f32[8,1,32]{2,1,0:T(1,128)S(1)} all-gather(f32[1,1,32]{2,1,0:T(1,128)S(1)} %get-tuple-element.329), channel_id=2, replica_groups=mesh['batch'=4,'tok'=8] {'tok'}, dimensions={0}, use_global_device_ids=true | all-gather | bytes 1152 | tf_op jit(solution)/shard_map/all_gather | solution.py:12
  28.2 68.8 %all-gather.13.cloned.1.call-done = f32[256,128,64]{1,2,0:T(8,128)} async-done(((f32[32,128,64]{1,2,0:T(8,128)}), f32[256,128,64]{1,2,0:T(8,128)}) %all-gather.13.cloned.1.call-update) | async-done | bytes 8388624 | tf_op jit(solution)/shard_map/all_gather | solution.py:12
  97.0 40.5 %while.18 = (s32[]{:T(128)}, f32[32,128,64]{2,1,0:T(8,128)}, s32[]{:T(128)}, f32[8,32]{1,0:T(8,128)S(1)}, f32[8,32,128,64]{2,3,1,0:T(8,128)}, /*index=5*/s32[]{:T(128)}, s32[]{:T(128)}) while((s32[]{:T(128)}, f32[32,128,64]{2,1,0:T(8,128)}, s32[]{:T(128)}, f32[8,32]{1,0:T(8,128)S(1)}, f32[8,32,128,64]{2,3,1,0:T(8,128)}, ...), condition=%wide.region_2.3_spmd.clone, body=%wide.region_1.2_spmd.clone.sunk | while | flops 1048580 | bytes 7340521 | solution.py:24
  98.9 1.7 fusion.80
  102.5 3.4 fusion.80
  105.9 1.6 constant_dynamic-slice_fusion.4
  108.2 3.2 fusion.80
  113.4 3.2 fusion.80
  118.6 3.3 fusion.80
  123.8 3.3 fusion.80
  129.0 3.3 fusion.80
  134.2 3.3 fusion.80
  137.5 2.5 fusion.14
  140.9 38.3 %all-gather.9.cloned.1.call-done = bf16[2048,2048]{1,0:T(8,128)(2,1)} async-done(((bf16[256,2048]{1,0:T(8,128)(2,1)}), bf16[2048,2048]{1,0:T(8,128)(2,1)}) %all-gather.9.cloned.1.call-update) | async-done | bytes 8388624 | tf_op jit(solution)/shard_map/all_gather | solution.py:141
  179.2 4.6 %fusion.3 = bf16[2,8,1,2048]{3,1,0,2:T(8,128)(2,1)S(1)} fusion(bf16[2048,2048]{1,0:T(8,128)(2,1)} %all-gather.9.cloned.1.call-done, bf16[16,2048]{1,0:T(8,128)(2,1)S(1)} %copy-done.8, f32[2048]{0:T(1024)S(1)} %copy-done.6, f32[16]{0:T(128)S(1)} %add_rsqrt_fusion.2, f32[16,2048]{1,0:T(8,128)S(1)} %reshape.330, bf16[16,2048]{1,0:T(8,128)(2,1)S(1)} %copy-done.2), kind=kOutput, calls=%fused_computation.11 | convolution fusion | flops 134610944 | bytes 8724544 | tf_op jit(solution)/shard_map/dot_general | solution.py:157
  184.5 3.4 all-to-all-start
  188.1 9.2 %all-to-all-done = bf16[1,8,2,2048]{3,2,0,1:T(2,128)(2,1)S(1)} async-done(((bf16[1,8,2,2048]{3,2,0,1:T(2,128)(2,1)}), bf16[1,8,2,2048]{3,2,0,1:T(2,128)(2,1)S(1)}, u32[]{:S(2)}, u32[]{:S(2)}) %all-to-all-start) | async-done | bytes 65568 | tf_op jit(solution)/shard_map/all_to_all | solution.py:163
  197.9 73.4 %all-gather.11.cloned.1.call-done = bf16[2048,2304]{1,0:T(8,128)(2,1)} async-done(((bf16[256,2304]{1,0:T(8,128)(2,1)}), bf16[2048,2304]{1,0:T(8,128)(2,1)}) %all-gather.11.cloned.1.call-update) | async-done | bytes 9437200 | tf_op jit(solution)/shard_map/all_gather | solution.py:142
  271.3 5.0 %convolution_convert_fusion = bf16[16,2304]{1,0:T(8,128)(2,1)S(1)} fusion(bf16[2048,2304]{1,0:T(8,128)(2,1)} %all-gather.11.cloned.1.call-done, f32[16,2048]{1,0:T(8,128)S(1)} %reshape.337, f32[2048]{0:T(1024)S(1)} %copy-done.5, f32[16]{0:T(128)S(1)} %rsqrt.29), kind=kOutput, calls=%fused_computation.8 | convolution fusion | flops 151130112 | bytes 9650240 | tf_op jit(solution)/shard_map/dot_general | solution.py:167
  276.4 2.2 collective-permute-start
  281.5 11.1 %all-gather.2 = f32[8,1,32]{2,1,0:T(1,128)S(1)} all-gather(f32[1,1,32]{2,1,0:T(1,128)S(1)} %get-tuple-element.325), channel_id=4, replica_groups=mesh['batch'=4,'tok'=8] {'tok'}, dimensions={0}, use_global_device_ids=true | all-gather | bytes 1152 | tf_op jit(solution)/shard_map/all_gather | solution.py:12
  293.5 70.5 %all-gather.15.cloned.1.call-done = f32[256,128,64]{1,2,0:T(8,128)} async-done(((f32[32,128,64]{1,2,0:T(8,128)}), f32[256,128,64]{1,2,0:T(8,128)}) %all-gather.15.cloned.1.call-update) | async-done | bytes 8388624 | tf_op jit(solution)/shard_map/all_gather | solution.py:12
  364.1 40.3 %while.19 = (s32[]{:T(128)}, f32[32,128,64]{2,1,0:T(8,128)}, s32[]{:T(128)}, f32[8,32]{1,0:T(8,128)S(1)}, f32[8,32,128,64]{2,3,1,0:T(8,128)}, /*index=5*/s32[]{:T(128)}, s32[]{:T(128)}) while((s32[]{:T(128)}, f32[32,128,64]{2,1,0:T(8,128)}, s32[]{:T(128)}, f32[8,32]{1,0:T(8,128)S(1)}, f32[8,32,128,64]{2,3,1,0:T(8,128)}, ...), condition=%wide.region_7.8_spmd.clone, body=%wide.region_6.7_spmd.clone.sunk | while | flops 1048580 | bytes 7340521 | solution.py:24
  366.0 1.7 fusion.81
  369.7 3.3 fusion.81
  374.9 3.3 fusion.81
  380.1 3.3 fusion.81
  385.4 3.3 fusion.81
  390.6 3.3 fusion.81
  395.8 3.3 fusion.81
  401.1 3.3 fusion.81
  404.4 2.5 fusion.20
  (141 shorter events, 44.8 us)
Async XLA Ops:
  6.5 191.0 %copy-start = (bf16[2048,32]{0,1:T(8,128)(2,1)S(1)}, bf16[2048,32]{0,1:T(8,128)(2,1)}, u32[]{:S(2)}) copy-start(bf16[2048,32]{0,1:T(8,128)(2,1)} %param.37) | copy-start | bytes 393220
  6.5 90.4 %all-gather.13.cloned.1.call-start = ((), (), s32[]{:S(2)}) async-start(), calls=%async_computation.3 | async-start | bytes 9437184 | tf_op jit(solution)/shard_map/all_gather | solution.py:12
  10.5 3.0 copy-start.3
  12.0 2.6 copy-start.14
  12.0 16.0 %copy-start.9 = (bf16[16,256]{1,0:T(8,128)(2,1)S(1)}, bf16[16,256]{1,0:T(8,128)(2,1)}, u32[]{:S(2)}) copy-start(bf16[16,256]{1,0:T(8,128)(2,1)} %param.25) | copy-start | bytes 24580
  12.1 167.1 %all-gather.9.cloned.1.call-start = ((), (), s32[]{:S(2)}) async-start(), calls=%async_computation.1 | async-start | bytes 9437184 | tf_op jit(solution)/shard_map/all_gather | solution.py:141
  12.8 258.5 %all-gather.11.cloned.1.call-start = ((), (), s32[]{:S(2)}) async-start(), calls=%async_computation.2 | async-start | bytes 10616832 | tf_op jit(solution)/shard_map/all_gather | solution.py:142
  137.5 2.6 copy-start.1
  137.5 2.6 copy-start.12
  137.5 3.1 copy-start.2
  137.5 41.7 %copy-start.6 = (f32[2048]{0:T(1024)S(1)}, f32[2048]{0:T(1024)}, u32[]{:S(2)}) copy-start(f32[2048]{0:T(1024)} %param.30) | copy-start | bytes 24580
  137.5 41.7 %copy-start.8 = (bf16[16,2048]{1,0:T(8,128)(2,1)S(1)}, bf16[16,2048]{1,0:T(8,128)(2,1)}, u32[]{:S(2)}) copy-start(bf16[16,2048]{1,0:T(8,128)(2,1)} %param.32) | copy-start | bytes 196612
  140.8 47.1 %copy-start.7 = (bf16[4,2304]{1,0:T(4,128)(2,1)S(1)}, bf16[4,2304]{1,0:T(4,128)(2,1)}, u32[]{:S(2)}) copy-start(bf16[4,2304]{1,0:T(4,128)(2,1)} %param.35) | copy-start | bytes 55300
  140.8 56.7 %copy-start.5 = (f32[2048]{0:T(1024)S(1)}, f32[2048]{0:T(1024)}, u32[]{:S(2)}) copy-start(f32[2048]{0:T(1024)} %param.33) | copy-start | bytes 24580
  140.9 56.7 %copy-start.13 = (f32[32]{0:T(128)S(1)}, f32[32]{0:T(128)}, u32[]{:S(2)}) copy-start(f32[32]{0:T(128)} %param.38) | copy-start | bytes 388
  184.5 12.8 %all-to-all-start = ((bf16[1,8,2,2048]{3,2,0,1:T(2,128)(2,1)}), bf16[1,8,2,2048]{3,2,0,1:T(2,128)(2,1)S(1)}, u32[]{:S(2)}, u32[]{:S(2)}) async-start(bf16[1,8,2,2048]{3,2,0,1:T(2,128)(2,1)} %bitcast.106), calls=%async_computation | async-start | bytes 131072 | tf_op jit(solution)/shard_map/all_to_all | solution.py:163
  187.9 176.2 %all-gather.15.cloned.1.call-start = ((), (), s32[]{:S(2)}) async-start(), calls=%async_computation.4 | async-start | bytes 9437184 | tf_op jit(solution)/shard_map/all_gather | solution.py:12
  197.9 81.5 %copy-start.10 = (f32[2304]{0:T(1024)S(1)}, f32[2304]{0:T(1024)}, u32[]{:S(2)}) copy-start(f32[2304]{0:T(1024)} %param.36) | copy-start | bytes 27652
  276.4 3.0 collective-permute-start
  404.4 2.6 copy-start.4
  404.4 2.6 copy-start.15
  404.4 3.2 copy-start.11
Sparse Core Ops, SparseCore 0:
  12.2 84.7 all-gather.12
  98.6 80.5 all-gather.8
  180.9 90.4 all-gather.10
  281.4 82.6 all-gather.14
where the time goes:
time: 416 us; the launch traced here: 415 us
  waiting for transfers between devices  262 us (63%)
  other arithmetic  53.7 us (13%)
  local copies, waits for them, and re-layouts  35.7 us (9%)
  blocking collectives  24.5 us (6%)
  matrix products  19 us (5%)
  between operations  13.5 us (3%)
  starting transfers between devices  5.64 us (1%)
    all_gather x2, waiting for transfers between devices, prefix(): everything = jax.tree.map(lambda part: lax.all_gather(part, axis), value)  139 us
    all_gather x1, waiting for transfers between devices, local(): lax.all_gather(in_weight, 'tok', axis=0, tiled=True)  73.4 us
    select_n x16, other arithmetic, hop(): return jax.tree.map(lambda a, b: jnp.where(reached, a, b), new, before)  49.4 us
    all_gather x1, waiting for transfers between devices, local(): lax.all_gather(out_weight, 'tok', axis=0, tiled=True)  38.3 us
    dynamic_slice x32, local copies, waits for them, and re-layouts, hop(): new = combine(before, jax.tree.map(lambda part: part[k], everything))  30.7 us
    all_gather x2, blocking collectives, prefix(): everything = jax.tree.map(lambda part: lax.all_gather(part, axis), value)  24.5 us
    all_to_all x1, waiting for transfers between devices, local(): lax.all_to_all(outgoing, 'tok', split_axis=1, concat_axis=1, tiled=True)  9.24 us
  transfers between devices with their start and end apart: 6, of which 6 were waited for; matrix products, arithmetic and copies ran while one was open for 13% of the time, Pallas kernels for 0%

commit v1 on v0

--- a/solution.py
+++ b/solution.py
@@ -1,6 +1,10 @@
+import functools
+
 import jax
 import jax.numpy as jnp
 from jax import lax
+from jax.experimental import pallas as pl
+from jax.experimental.pallas import tpu as pltpu
 from jax.sharding import PartitionSpec as P
 
 KC = 4
@@ -190,6 +194,378 @@
     return rms_scale(scanned_two, final_gain).astype(jnp.bfloat16)
 
 
+MESH = pl.DeviceIdType.MESH
+BF = jnp.bfloat16
+F32 = jnp.float32
+INNER_K, BC_K, RAW_K, GATE_K, RES_K, SQ1_K, OUT_K, SQ2_K, VAL_K, PROJ_K, FIN_K = range(11)
+KINDS = 11
+
+
+def softplus(x):
+    return jnp.maximum(x, 0.0) + jnp.log1p(jnp.exp(-jnp.abs(x)))
+
+
+def as_column(row):
+    rows = row.shape[1]
+    return jnp.broadcast_to(row, (rows, rows)).T[:, 0:1]
+
+
+def as_rows(column):
+    rows = column.shape[0]
+    return jnp.broadcast_to(column, (rows, rows)).T[0:8]
+
+
+def ssd_heads(values, write_side, read_side, steps, rates, skips, heads, tmp):
+    rows, width = values.shape
+    head = width // heads
+    at = lax.broadcasted_iota(jnp.int32, (rows, rows), 0)
+    source = lax.broadcasted_iota(jnp.int32, (rows, rows), 1)
+    ahead = (at <= source).astype(F32)
+    cumulative = jnp.dot(
+        -rates * steps, ahead, precision=lax.Precision.HIGHEST, preferred_element_type=F32
+    )
+    tmp[0:8, :] = cumulative
+    columns = tmp[...].T
+    scores = lax.dot_general(
+        read_side, write_side, (((1,), (1,)), ((), ())), preferred_element_type=F32
+    )
+    lower = source <= at
+    mixing = []
+    for h in range(heads):
+        gap = columns[:, h : h + 1] - cumulative[h : h + 1, :]
+        decay = jnp.exp(jnp.where(lower, gap, -1e30))
+        mixing.append((scores * decay * steps[h : h + 1, :]).astype(BF))
+    product = jnp.dot(jnp.concatenate(mixing, axis=0), values, preferred_element_type=F32)
+    owner = lax.broadcasted_iota(jnp.int32, (rows, width), 1) // head
+    wide = values.astype(F32)
+    result = jnp.zeros((rows, width), F32)
+    for h in range(heads):
+        part = product[h * rows : (h + 1) * rows] + skips[h : h + 1, :] * wide
+        result = jnp.where(owner == h, part, result)
+    return result
+
+
+def fused(
+    peers,
+    heads,
+    inner,
+    gate,
+    bc,
+    raw,
+    rate_one,
+    bias_one,
+    skip_one,
+    norm_gain,
+    out_hbm,
+    residual,
+    pre_gain,
+    in_hbm,
+    conv_weight,
+    conv_bias,
+    step_weight,
+    bias_two,
+    rate_two,
+    skip_two,
+    final_gain,
+    result,
+    out_w,
+    in_w,
+    inner_all,
+    gate_all,
+    bc_all,
+    raw_all,
+    res_all,
+    out_tx,
+    out_rx,
+    sq1_tx,
+    sq1_rx,
+    val_tx,
+    val_rx,
+    proj_tx,
+    proj_rx,
+    sq2_tx,
+    sq2_rx,
+    fin_tx,
+    fin,
+    tmp,
+    load_sem,
+    send_sem,
+    recv_sem,
+):
+    tok_rows, inner_width = inner.shape
+    rows = tok_rows * peers
+    slab = inner_width // peers
+    state = bc.shape[1] // 2
+    total_heads = heads * peers
+    me = lax.axis_index("tok")
+    order = [peers // 2]
+    for d in range(1, peers // 2):
+        order += [peers // 2 - d, peers // 2 + d]
+
+    def peer(d):
+        return lax.rem(me + d, peers)
+
+    def at(index, size):
+        return pl.ds(pl.multiple_of(index * size, size), size)
+
+    flights = []
+
+    def send(kind, d, src, dst):
+        copy = pltpu.make_async_remote_copy(
+            src_ref=src,
+            dst_ref=dst,
+            send_sem=send_sem.at[kind, d],
+            recv_sem=recv_sem.at[kind, d],
+            device_id={"tok": peer(d)},
+            device_id_type=MESH,
+        )
+        copy.start()
+        flights.append(copy)
+        return copy
+
+    load_out = pltpu.make_async_copy(out_hbm, out_w, load_sem.at[0])
+    load_in = pltpu.make_async_copy(in_hbm, in_w, load_sem.at[1])
+    load_out.start()
+    load_in.start()
+    barrier = pltpu.get_barrier_semaphore()
+    for d in range(1, peers):
+        pl.semaphore_signal(barrier, inc=1, device_id={"tok": peer(d)}, device_id_type=MESH)
+    mine = at(me, slab)
+    my_rows = at(me, tok_rows)
+    inner_all[my_rows, :] = inner[:, mine]
+    gate_all[my_rows, :] = gate[:, mine]
+    res_all[my_rows, :] = residual[:, mine]
+    bc_all[my_rows, :] = bc[...]
+    raw_all[my_rows, :] = raw[...]
+    tmp[...] = jnp.zeros_like(tmp)
+    for index, ref in enumerate((rate_one, bias_one, skip_one, rate_two, bias_two, skip_two)):
+        tmp[index : index + 1, 0:total_heads] = ref[...]
+    lanes = tmp.shape[1]
+    turn = lax.rem(lanes - me * heads, lanes)
+    params = pltpu.roll(tmp[...], turn, 1).T
+    pl.semaphore_wait(barrier, peers - 1)
+
+    first = {}
+    for d in order:
+        first[RAW_K, d] = send(RAW_K, d, raw, raw_all.at[my_rows, :])
+        first[BC_K, d] = send(BC_K, d, bc, bc_all.at[my_rows, :])
+        first[INNER_K, d] = send(
+            INNER_K, d, inner.at[:, at(peer(d), slab)], inner_all.at[my_rows, :]
+        )
+    for d in order:
+        first[GATE_K, d] = send(GATE_K, d, gate.at[:, at(peer(d), slab)], gate_all.at[my_rows, :])
+    for d in order:
+        first[RES_K, d] = send(RES_K, d, residual.at[:, at(peer(d), slab)], res_all.at[my_rows, :])
+
+    def arrived(copies, *kinds):
+        for kind in kinds:
+            for d in order:
+                copies[kind, d].wait_recv()
+
+    arrived(first, RAW_K)
+    tmp[...] = jnp.zeros_like(tmp)
+    tmp[:, 0:total_heads] = raw_all[...]
+    steps = softplus(pltpu.roll(tmp[...], turn, 1).T[0:8] + params[0:8, 1:2])
+    arrived(first, BC_K, INNER_K)
+    scanned = ssd_heads(
+        inner_all[...],
+        bc_all[:, 0:state],
+        bc_all[:, state : 2 * state],
+        steps,
+        params[0:8, 0:1],
+        params[0:8, 2:3],
+        heads,
+        tmp,
+    )
+    arrived(first, GATE_K)
+    gated = scanned * jax.nn.silu(gate_all[...].astype(F32))
+    sq1_tx[...] = as_rows(jnp.sum(gated * gated, axis=1, keepdims=True))
+    second = {}
+    for d in order:
+        second[SQ1_K, d] = send(SQ1_K, d, sq1_tx, sq1_rx.at[d])
+    scaled = (gated * norm_gain[:, mine]).astype(BF)
+    load_out.wait()
+    for d in order:
+        out_tx[d] = jnp.dot(
+            scaled, out_w[:, at(peer(d), slab)], preferred_element_type=F32
+        ).astype(BF)
+        second[OUT_K, d] = send(OUT_K, d, out_tx.at[d], out_rx.at[d])
+    hidden = jnp.dot(scaled, out_w[:, mine], preferred_element_type=F32)
+    arrived(first, RES_K)
+    arrived(second, SQ1_K)
+    squares = sq1_tx[...]
+    for d in order:
+        squares = squares + sq1_rx[d]
+    scale = as_column(lax.rsqrt(squares[0:1] / inner_width + 1e-05))
+    for d in order:
+        second[OUT_K, d].wait_recv()
+        hidden = hidden + out_rx[d].astype(F32)
+    hidden = (res_all[...].astype(F32) + scale * hidden).astype(BF)
+    to = lax.broadcasted_iota(jnp.int32, (rows, rows), 0)
+    raster = lax.broadcasted_iota(jnp.int32, (rows, rows), 1)
+    moved = (raster % peers) * (rows // peers) + raster // peers
+    hidden = jnp.dot((to == moved).astype(BF), hidden, preferred_element_type=F32)
+
+    width = in_w.shape[1]
+    pre = (hidden * pre_gain[:, mine]).astype(BF)
+    tmp[...] = jnp.zeros_like(tmp)
+    tmp[:, 0:total_heads] = jnp.dot(pre, step_weight[mine, :], preferred_element_type=F32)
+    logits = tmp[...].T
+    squares = as_rows(jnp.sum(hidden * hidden, axis=1, keepdims=True))
+    for p in range(peers):
+        sq2_tx[p, 0:heads, :] = logits[p * heads : (p + 1) * heads]
+        sq2_tx[p, heads:8, :] = squares[heads:8]
+    third = {}
+    for d in order:
+        third[SQ2_K, d] = send(SQ2_K, d, sq2_tx.at[peer(d)], sq2_rx.at[d])
+    load_in.wait()
+    proj = jnp.dot(pre, in_w[:, inner_width:width], preferred_element_type=F32)
+    proj_tx[...] = proj.astype(BF)
+    for d in order:
+        third[PROJ_K, d] = send(PROJ_K, d, proj_tx, proj_rx.at[d])
+    for d in order:
+        val_tx[d] = jnp.dot(pre, in_w[:, at(peer(d), slab)], preferred_element_type=F32).astype(BF)
+        third[VAL_K, d] = send(VAL_K, d, val_tx.at[d], val_rx.at[d])
+    value = jnp.dot(pre, in_w[:, mine], preferred_element_type=F32)
+    arrived(third, SQ2_K)
+    gathered = sq2_tx[me]
+    for d in order:
+        gathered = gathered + sq2_rx[d]
+    scale_row = lax.rsqrt(gathered[heads : heads + 1] / inner_width + 1e-05)
+    scale = as_column(scale_row)
+    steps = softplus(scale_row * gathered + params[0:8, 4:5])
+
+    def convolve(projected, columns):
+        projected = projected.astype(BF).astype(F32)
+        taps = conv_weight[:, columns].astype(F32)
+        place = lax.broadcasted_iota(jnp.int32, projected.shape, 0)
+        total = conv_bias[:, columns]
+        for offset in range(KC):
+            back = KC - 1 - offset
+            term = projected
+            if back:
+                term = jnp.where(place < back, 0.0, pltpu.roll(projected, back, 0))
+            total = total + taps[offset : offset + 1] * term
+        return jax.nn.silu(total).astype(BF)
+
+    for d in order:
+        third[PROJ_K, d].wait_recv()
+        proj = proj + proj_rx[d].astype(F32)
+    both = convolve(scale * proj, slice(inner_width, width))
+    for d in order:
+        third[VAL_K, d].wait_recv()
+        value = value + val_rx[d].astype(F32)
+    scanned = ssd_heads(
+        convolve(scale * value, mine),
+        both[:, 0:state],
+        both[:, state : 2 * state],
+        steps,
+        params[0:8, 3:4],
+        params[0:8, 5:6],
+        heads,
+        tmp,
+    ).astype(BF)
+    fin_tx[...] = scanned
+    last = {}
+    for d in order:
+        last[FIN_K, d] = send(FIN_K, d, fin_tx.at[at(peer(d), tok_rows), :], fin.at[:, mine])
+    fin[:, mine] = fin_tx[my_rows, :]
+    arrived(last, FIN_K)
+    result[...] = rms_scale(fin[...].astype(F32), final_gain[0]).astype(BF)
+    for copy in flights:
+        copy.wait_send()
+
+
+def fused_local(peers, *args):
+    (inner, gate, bc, raw, rate_one, bias_one, skip_one, norm_gain, out_w, residual) = args[:10]
+    (pre_gain, in_w, conv_w, conv_bias, step_w, bias_two, rate_two, skip_two, final_gain) = args[10:]
+    tok_rows, inner_width = inner.shape
+    heads = rate_one.shape[0] // peers
+    rows, slab = (tok_rows * peers, inner_width // peers)
+    state2 = bc.shape[1]
+
+    def flat(vector):
+        return vector.reshape(1, vector.shape[0])
+
+    vmem = pl.BlockSpec(memory_space=pltpu.VMEM)
+    anywhere = pl.BlockSpec(memory_space=pl.ANY)
+    specs = [vmem] * 19
+    specs[8] = anywhere
+    specs[11] = anywhere
+    return pl.pallas_call(
+        functools.partial(fused, peers, heads),
+        out_shape=jax.ShapeDtypeStruct((tok_rows, inner_width), BF),
+        in_specs=specs,
+        out_specs=vmem,
+        scratch_shapes=[
+            pltpu.VMEM(out_w.shape, BF),
+            pltpu.VMEM(in_w.shape, BF),
+            pltpu.VMEM((rows, slab), BF),
+            pltpu.VMEM((rows, slab), BF),
+            pltpu.VMEM((rows, state2), BF),
+            pltpu.VMEM((rows, raw.shape[1]), F32),
+            pltpu.VMEM((rows, slab), BF),
+            pltpu.VMEM((peers, rows, slab), BF),
+            pltpu.VMEM((peers, rows, slab), BF),
+            pltpu.VMEM((8, rows), F32),
+            pltpu.VMEM((peers, 8, rows), F32),
+            pltpu.VMEM((peers, rows, slab), BF),
+            pltpu.VMEM((peers, rows, slab), BF),
+            pltpu.VMEM((rows, state2), BF),
+            pltpu.VMEM((peers, rows, state2), BF),
+            pltpu.VMEM((peers, 8, rows), F32),
+            pltpu.VMEM((peers, 8, rows), F32),
+            pltpu.VMEM((rows, slab), BF),
+            pltpu.VMEM((tok_rows, inner_width), BF),
+            pltpu.VMEM((rows, rows), F32),
+            pltpu.SemaphoreType.DMA((2,)),
+            pltpu.SemaphoreType.DMA((KINDS, peers)),
+            pltpu.SemaphoreType.DMA((KINDS, peers)),
+        ],
+        compiler_params=pltpu.CompilerParams(
+            collective_id=0, has_side_effects=True, vmem_limit_bytes=40 * 1024 * 1024
+        ),
+    )(
+        inner,
+        gate,
+        bc,
+        raw,
+        flat(rate_one),
+        flat(bias_one),
+        flat(skip_one),
+        flat(norm_gain),
+        out_w,
+        residual,
+        flat(pre_gain),
+        in_w,
+        conv_w,
+        flat(conv_bias),
+        step_w,
+        flat(bias_two),
+        flat(rate_two),
+        flat(skip_two),
+        flat(final_gain),
+    )
+
+
+def local_step(peers, *args):
+    inner, bc, rates = (args[0], args[2], args[4])
+    tok_rows, inner_width = inner.shape
+    heads = rates.shape[0]
+    fits = (
+        tok_rows * peers == 128
+        and tok_rows % 16 == 0
+        and tok_rows % peers == 0
+        and heads % peers == 0
+        and heads // peers < 8
+        and heads <= 128
+        and inner_width % (128 * peers) == 0
+        and args[9].shape[1] == inner_width
+        and bc.shape[1] == 256
+    )
+    return fused_local(peers, *args) if fits else local(*args)
+
+
 def solution(mesh):
     placed = (
         P(("batch", "tok"), None),
@@ -213,5 +589,5 @@
         P(),
     )
     return jax.shard_map(
-        local, mesh=mesh, in_specs=placed, out_specs=P(("batch", "tok"), None), check_vma=False
-    )
+        functools.partial(local_step, mesh.shape["tok"]), mesh=mesh, in_specs=placed, out_specs=P(("batch", "tok"), None), check_vma=False
+    )

time: 416 us -> 74.3 us (0.18)
  waiting for transfers between devices: 262 us -> 0 us
  Pallas kernels: 0 us -> 57.8 us
  other arithmetic: 53.7 us -> 0 us
  blocking collectives: 24.5 us -> 0 us
  local copies, waits for them, and re-layouts: 35.7 us -> 15.7 us
  matrix products: 19 us -> 0 us
  between operations: 13.5 us -> 0.04 us
  starting transfers between devices: 5.64 us -> 0 us
    all_gather x4 -> x0, waiting for transfers between devices: 251 us -> none  [the longest x2 139 us: prefix(): everything = jax.tree.map(lambda part: lax.all_gather(part, axis), value)]
    pallas_call x0 -> x1, Pallas kernels: none -> 57.8 us  [fused_local(): pl.pallas_call(functools.partial(fused, peers, heads), out_shape=jax.Shap...]
    select_n x16 -> x0, other arithmetic: 49.4 us -> none  [hop(): return jax.tree.map(lambda a, b: jnp.where(reached, a, b), new, before)]
    dynamic_slice x32 -> x0, local copies, waits for them, and re-layouts: 30.7 us -> none  [hop(): new = combine(before, jax.tree.map(lambda part: part[k], everything))]
    all_gather x2 -> x0, blocking collectives: 24.5 us -> none  [prefix(): everything = jax.tree.map(lambda part: lax.all_gather(part, axis), value)]
    dot_general x11 -> x0, matrix products: 19 us -> none  [the longest x2 5.07 us: ssd_local(): jnp.einsum('btn,bhnp->bthp', read_blocks.astype(jnp.float32), entry, prec...]
    unnamed x32 -> x36, local copies, waits for them, and re-layouts: 0.07 us -> 14.9 us
    all_to_all x1 -> x0, waiting for transfers between devices: 9.24 us -> none  [local(): lax.all_to_all(outgoing, 'tok', split_axis=1, concat_axis=1, tiled=True)]
  transfers between devices with their start and end apart: 6 -> 0, of which waited for: 6 -> 0; matrix products, arithmetic and copies ran while one was open for 13% -> 0% of each run, Pallas kernels for 0% -> 0%
where the time goes in v1:
time: 74.3 us; the launch traced here: 73.5 us
  Pallas kernels  57.8 us (78%)
  local copies, waits for them, and re-layouts  15.7 us (21%)
    pallas_call x1, Pallas kernels, fused_local(): pl.pallas_call(functools.partial(fused, peers, heads), out_shape=jax.Shap...  57.8 us
    unnamed x36, local copies, waits for them, and re-layouts  14.9 us

profile of v1, /device:TPU:0, one launch (start us, length us, event | category | flops | bytes accessed | tf_op | source)
XLA Modules:
  0.0 73.5 jit_solution(2049785666435011636)
XLA Ops:
  0.0 0.7 reshape.35.conv_bias
  0.7 1.2 %copy.20.step_weight = bf16[2048,32]{1,0:T(8,128)(2,1)S(1)} copy(bf16[2048,32]{0,1:T(8,128)(2,1)} %param.33) | data formatting | bytes 262144 | tf_op args[14]
  1.9 0.0 copy-start
  1.9 1.3 %copy-done = bf16[256,2304]{1,0:T(8,128)(2,1)S(1)} copy-done((bf16[256,2304]{1,0:T(8,128)(2,1)S(1)}, bf16[256,2304]{1,0:T(8,128)(2,1)}, u32[]{:S(2)}) %copy-start) | copy-done | bytes 1179672
  3.2 0.0 copy-start.1
  3.2 1.2 %copy-done.1 = bf16[256,2048]{1,0:T(8,128)(2,1)S(1)} copy-done((bf16[256,2048]{1,0:T(8,128)(2,1)S(1)}, bf16[256,2048]{1,0:T(8,128)(2,1)}, u32[]{:S(2)}) %copy-start.1) | copy-done | bytes 1048600
  4.4 0.0 copy-start.2
  4.4 0.8 %copy-done.2 = bf16[16,2048]{1,0:T(8,128)(2,1)S(1)} copy-done((bf16[16,2048]{1,0:T(8,128)(2,1)S(1)}, bf16[16,2048]{1,0:T(8,128)(2,1)}, u32[]{:S(2)}) %copy-start.2) | copy-done | bytes 65560
  5.2 0.0 copy-start.3
  5.2 0.8 %copy-done.3 = bf16[16,2048]{1,0:T(8,128)(2,1)S(1)} copy-done((bf16[16,2048]{1,0:T(8,128)(2,1)S(1)}, bf16[16,2048]{1,0:T(8,128)(2,1)}, u32[]{:S(2)}) %copy-start.3) | copy-done | bytes 65560
  6.1 0.0 copy-start.4
  6.1 0.8 %copy-done.4 = bf16[16,2048]{1,0:T(8,128)(2,1)S(1)} copy-done((bf16[16,2048]{1,0:T(8,128)(2,1)S(1)}, bf16[16,2048]{1,0:T(8,128)(2,1)}, u32[]{:S(2)}) %copy-start.4) | copy-done | bytes 65560
  6.9 0.0 copy-start.5
  6.9 0.7 copy-done.5
  7.6 0.0 copy-start.6
  7.6 0.7 copy-done.6
  8.3 0.0 copy-start.7
  8.3 0.7 copy-done.7
  9.0 0.0 copy-start.8
  9.0 0.7 copy-done.8
  9.7 0.0 copy-start.9
  9.7 0.7 copy-done.9
  10.4 0.0 copy-start.10
  10.4 0.7 copy-done.10
  11.1 0.7 copy-done.11
  11.8 0.7 copy-done.12
  12.4 0.7 copy-done.13
  13.1 0.7 copy-done.14
  13.8 0.7 copy-done.15
  14.4 0.7 copy-done.16
  15.1 57.8 %shard_map.181 = bf16[16,2048]{1,0:T(8,128)(2,1)S(1)} custom-call(bf16[16,2048]{1,0:T(8,128)(2,1)S(1)} %copy-done.2, bf16[16,2048]{1,0:T(8,128)(2,1)S(1)} %copy-done.3, bf16[16,256]{1,0:T(8,128)(2,1)S(1)} %copy-done.6, f32[16,32]{1,0:T(8,128)S(1)} %copy-done.7, f32[1,32]{1,0:T(1,128)S(1)} %bitcast.12, f32[1,32]{1,0:T(1,128)S(1)} %bitcast.13, ...), custom_call_target="tpu_custom_call" | custom-call | tf_op jit(solution)/shard_map/pallas_call | solution.py:495
  72.9 0.6 copy.22
  (6 shorter events, 0.0 us)
Async XLA Ops:
  1.9 1.3 %copy-start = (bf16[256,2304]{1,0:T(8,128)(2,1)S(1)}, bf16[256,2304]{1,0:T(8,128)(2,1)}, u32[]{:S(2)}) copy-start(bf16[256,2304]{1,0:T(8,128)(2,1)} %in_hbm.1) | copy-start | bytes 3538948
  3.2 1.2 %copy-start.1 = (bf16[256,2048]{1,0:T(8,128)(2,1)S(1)}, bf16[256,2048]{1,0:T(8,128)(2,1)}, u32[]{:S(2)}) copy-start(bf16[256,2048]{1,0:T(8,128)(2,1)} %out_hbm.1) | copy-start | bytes 3145732
  4.4 0.8 %copy-start.2 = (bf16[16,2048]{1,0:T(8,128)(2,1)S(1)}, bf16[16,2048]{1,0:T(8,128)(2,1)}, u32[]{:S(2)}) copy-start(bf16[16,2048]{1,0:T(8,128)(2,1)} %inner.1) | copy-start | bytes 196612
  5.2 0.8 %copy-start.3 = (bf16[16,2048]{1,0:T(8,128)(2,1)S(1)}, bf16[16,2048]{1,0:T(8,128)(2,1)}, u32[]{:S(2)}) copy-start(bf16[16,2048]{1,0:T(8,128)(2,1)} %gate.1) | copy-start | bytes 196612
  6.1 0.8 %copy-start.4 = (bf16[16,2048]{1,0:T(8,128)(2,1)S(1)}, bf16[16,2048]{1,0:T(8,128)(2,1)}, u32[]{:S(2)}) copy-start(bf16[16,2048]{1,0:T(8,128)(2,1)} %residual.1) | copy-start | bytes 196612
  6.9 0.7 copy-start.5
  7.6 0.7 copy-start.6
  8.3 0.7 copy-start.7
  9.0 0.7 copy-start.8
  9.7 0.7 copy-start.9
  10.4 0.7 copy-start.10
  11.1 0.7 copy-start.11
  11.8 0.7 copy-start.12
  12.4 0.7 copy-start.13
  13.1 0.7 copy-start.14
  13.8 0.7 copy-start.15
  14.4 0.7 copy-start.16

commit v2 on v1

--- a/solution.py
+++ b/solution.py
@@ -197,8 +197,9 @@
 MESH = pl.DeviceIdType.MESH
 BF = jnp.bfloat16
 F32 = jnp.float32
-INNER_K, BC_K, RAW_K, GATE_K, RES_K, SQ1_K, OUT_K, SQ2_K, VAL_K, PROJ_K, FIN_K = range(11)
-KINDS = 11
+INNER_K, BC_K, RAW_K, GATE_K, RES_K, SQ1_K, OUT_K, SQ2_K, VAL_K, PROJ_K, SPREAD_K, FIN_K = range(12)
+KINDS = 12
+LOADS = 19
 
 
 def softplus(x):
@@ -245,53 +246,14 @@
     return result
 
 
-def fused(
-    peers,
-    heads,
-    inner,
-    gate,
-    bc,
-    raw,
-    rate_one,
-    bias_one,
-    skip_one,
-    norm_gain,
-    out_hbm,
-    residual,
-    pre_gain,
-    in_hbm,
-    conv_weight,
-    conv_bias,
-    step_weight,
-    bias_two,
-    rate_two,
-    skip_two,
-    final_gain,
-    result,
-    out_w,
-    in_w,
-    inner_all,
-    gate_all,
-    bc_all,
-    raw_all,
-    res_all,
-    out_tx,
-    out_rx,
-    sq1_tx,
-    sq1_rx,
-    val_tx,
-    val_rx,
-    proj_tx,
-    proj_rx,
-    sq2_tx,
-    sq2_rx,
-    fin_tx,
-    fin,
-    tmp,
-    load_sem,
-    send_sem,
-    recv_sem,
-):
+def fused(peers, heads, *refs):
+    (inner, gate, bc, raw), (residual,), small_hbm = (refs[0:4], refs[4:5], refs[5:19])
+    result, small = (refs[19], refs[20:34])
+    (rate_one, bias_one, skip_one, rate_two, bias_two, skip_two) = small[0:6]
+    (out_w, norm_gain, pre_gain, in_w, step_weight, conv_weight, conv_bias, final_gain) = small[6:14]
+    (inner_all, gate_all, bc_all, raw_all, res_all, out_tx, out_rx, sq1_tx, sq1_rx) = refs[34:43]
+    (val_tx, val_rx, proj_tx, proj_rx, spread_tx, proj_all, sq2_tx, sq2_rx) = refs[43:51]
+    (fin_tx, fin, tmp, load_sem, send_sem, recv_sem) = refs[51:57]
     tok_rows, inner_width = inner.shape
     rows = tok_rows * peers
     slab = inner_width // peers
@@ -323,49 +285,60 @@
         flights.append(copy)
         return copy
 
-    load_out = pltpu.make_async_copy(out_hbm, out_w, load_sem.at[0])
-    load_in = pltpu.make_async_copy(in_hbm, in_w, load_sem.at[1])
-    load_out.start()
-    load_in.start()
+    mine = at(me, slab)
+    my_rows = at(me, tok_rows)
+    loads = [
+        pltpu.make_async_copy(source, target, load_sem.at[index])
+        for index, (source, target) in enumerate(
+            [
+                (raw, raw_all.at[my_rows, :]),
+                (bc, bc_all.at[my_rows, :]),
+                (inner.at[:, mine], inner_all.at[my_rows, :]),
+                (gate.at[:, mine], gate_all.at[my_rows, :]),
+                (residual.at[:, mine], res_all.at[my_rows, :]),
+                *zip(small_hbm, small),
+            ]
+        )
+    ]
+    for load in loads:
+        load.start()
     barrier = pltpu.get_barrier_semaphore()
     for d in range(1, peers):
         pl.semaphore_signal(barrier, inc=1, device_id={"tok": peer(d)}, device_id_type=MESH)
-    mine = at(me, slab)
-    my_rows = at(me, tok_rows)
-    inner_all[my_rows, :] = inner[:, mine]
-    gate_all[my_rows, :] = gate[:, mine]
-    res_all[my_rows, :] = residual[:, mine]
-    bc_all[my_rows, :] = bc[...]
-    raw_all[my_rows, :] = raw[...]
+    pl.semaphore_wait(barrier, peers - 1)
+
+    first = {}
+    for d in order:
+        first[RAW_K, d] = send(RAW_K, d, raw, raw_all.at[my_rows, :])
+        first[BC_K, d] = send(BC_K, d, bc, bc_all.at[my_rows, :])
+        first[INNER_K, d] = send(
+            INNER_K, d, inner.at[:, at(peer(d), slab)], inner_all.at[my_rows, :]
+        )
+    for d in order:
+        first[GATE_K, d] = send(GATE_K, d, gate.at[:, at(peer(d), slab)], gate_all.at[my_rows, :])
+    for d in order:
+        first[RES_K, d] = send(RES_K, d, residual.at[:, at(peer(d), slab)], res_all.at[my_rows, :])
+
+    def arrived(copies, *kinds):
+        for kind in kinds:
+            for d in order:
+                copies[kind, d].wait_recv()
+
     tmp[...] = jnp.zeros_like(tmp)
+    for load in loads[5:11]:
+        load.wait()
     for index, ref in enumerate((rate_one, bias_one, skip_one, rate_two, bias_two, skip_two)):
         tmp[index : index + 1, 0:total_heads] = ref[...]
     lanes = tmp.shape[1]
     turn = lax.rem(lanes - me * heads, lanes)
     params = pltpu.roll(tmp[...], turn, 1).T
-    pl.semaphore_wait(barrier, peers - 1)
-
-    first = {}
-    for d in order:
-        first[RAW_K, d] = send(RAW_K, d, raw, raw_all.at[my_rows, :])
-        first[BC_K, d] = send(BC_K, d, bc, bc_all.at[my_rows, :])
-        first[INNER_K, d] = send(
-            INNER_K, d, inner.at[:, at(peer(d), slab)], inner_all.at[my_rows, :]
-        )
-    for d in order:
-        first[GATE_K, d] = send(GATE_K, d, gate.at[:, at(peer(d), slab)], gate_all.at[my_rows, :])
-    for d in order:
-        first[RES_K, d] = send(RES_K, d, residual.at[:, at(peer(d), slab)], res_all.at[my_rows, :])
-
-    def arrived(copies, *kinds):
-        for kind in kinds:
-            for d in order:
-                copies[kind, d].wait_recv()
-
+    tmp[...] = jnp.zeros_like(tmp)
+    loads[0].wait()
     arrived(first, RAW_K)
-    tmp[...] = jnp.zeros_like(tmp)
     tmp[:, 0:total_heads] = raw_all[...]
     steps = softplus(pltpu.roll(tmp[...], turn, 1).T[0:8] + params[0:8, 1:2])
+    loads[1].wait()
+    loads[2].wait()
     arrived(first, BC_K, INNER_K)
     scanned = ssd_heads(
         inner_all[...],
@@ -377,20 +350,23 @@
         heads,
         tmp,
     )
+    loads[3].wait()
     arrived(first, GATE_K)
     gated = scanned * jax.nn.silu(gate_all[...].astype(F32))
     sq1_tx[...] = as_rows(jnp.sum(gated * gated, axis=1, keepdims=True))
     second = {}
     for d in order:
         second[SQ1_K, d] = send(SQ1_K, d, sq1_tx, sq1_rx.at[d])
+    loads[11].wait()
+    loads[12].wait()
     scaled = (gated * norm_gain[:, mine]).astype(BF)
-    load_out.wait()
     for d in order:
         out_tx[d] = jnp.dot(
             scaled, out_w[:, at(peer(d), slab)], preferred_element_type=F32
         ).astype(BF)
         second[OUT_K, d] = send(OUT_K, d, out_tx.at[d], out_rx.at[d])
     hidden = jnp.dot(scaled, out_w[:, mine], preferred_element_type=F32)
+    loads[4].wait()
     arrived(first, RES_K)
     arrived(second, SQ1_K)
     squares = sq1_tx[...]
@@ -407,10 +383,12 @@
     hidden = jnp.dot((to == moved).astype(BF), hidden, preferred_element_type=F32)
 
     width = in_w.shape[1]
+    for load in loads[13:19]:
+        load.wait()
     pre = (hidden * pre_gain[:, mine]).astype(BF)
-    tmp[...] = jnp.zeros_like(tmp)
-    tmp[:, 0:total_heads] = jnp.dot(pre, step_weight[mine, :], preferred_element_type=F32)
-    logits = tmp[...].T
+    logits = lax.dot_general(
+        step_weight[:, mine], pre, (((1,), (1,)), ((), ())), preferred_element_type=F32
+    )
     squares = as_rows(jnp.sum(hidden * hidden, axis=1, keepdims=True))
     for p in range(peers):
         sq2_tx[p, 0:heads, :] = logits[p * heads : (p + 1) * heads]
@@ -418,14 +396,30 @@
     third = {}
     for d in order:
         third[SQ2_K, d] = send(SQ2_K, d, sq2_tx.at[peer(d)], sq2_rx.at[d])
-    load_in.wait()
-    proj = jnp.dot(pre, in_w[:, inner_width:width], preferred_element_type=F32)
-    proj_tx[...] = proj.astype(BF)
-    for d in order:
-        third[PROJ_K, d] = send(PROJ_K, d, proj_tx, proj_rx.at[d])
-    for d in order:
+    proj_tx[...] = jnp.dot(
+        pre, in_w[:, inner_width:width], preferred_element_type=F32
+    ).astype(BF)
+    for d in order:
+        third[PROJ_K, d] = send(
+            PROJ_K, d, proj_tx.at[at(peer(d), tok_rows), :], proj_rx.at[d]
+        )
+
+    def send_values(d):
         val_tx[d] = jnp.dot(pre, in_w[:, at(peer(d), slab)], preferred_element_type=F32).astype(BF)
         third[VAL_K, d] = send(VAL_K, d, val_tx.at[d], val_rx.at[d])
+
+    for d in order[0:4]:
+        send_values(d)
+    proj = proj_tx[my_rows, :].astype(F32)
+    for d in order:
+        third[PROJ_K, d].wait_recv()
+        proj = proj + proj_rx[d].astype(F32)
+    spread_tx[...] = proj.astype(BF)
+    for d in order:
+        third[SPREAD_K, d] = send(SPREAD_K, d, spread_tx, proj_all.at[my_rows, :])
+    proj_all[my_rows, :] = spread_tx[...]
+    for d in order[4:]:
+        send_values(d)
     value = jnp.dot(pre, in_w[:, mine], preferred_element_type=F32)
     arrived(third, SQ2_K)
     gathered = sq2_tx[me]
@@ -436,7 +430,6 @@
     steps = softplus(scale_row * gathered + params[0:8, 4:5])
 
     def convolve(projected, columns):
-        projected = projected.astype(BF).astype(F32)
         taps = conv_weight[:, columns].astype(F32)
         place = lax.broadcasted_iota(jnp.int32, projected.shape, 0)
         total = conv_bias[:, columns]
@@ -448,10 +441,8 @@
             total = total + taps[offset : offset + 1] * term
         return jax.nn.silu(total).astype(BF)
 
-    for d in order:
-        third[PROJ_K, d].wait_recv()
-        proj = proj + proj_rx[d].astype(F32)
-    both = convolve(scale * proj, slice(inner_width, width))
+    arrived(third, SPREAD_K)
+    both = convolve(scale * proj_all[...].astype(F32), slice(inner_width, width))
     for d in order:
         third[VAL_K, d].wait_recv()
         value = value + val_rx[d].astype(F32)
@@ -487,65 +478,49 @@
     def flat(vector):
         return vector.reshape(1, vector.shape[0])
 
-    vmem = pl.BlockSpec(memory_space=pltpu.VMEM)
-    anywhere = pl.BlockSpec(memory_space=pl.ANY)
-    specs = [vmem] * 19
-    specs[8] = anywhere
-    specs[11] = anywhere
+    big = (inner, gate, bc, raw, residual)
+    small = tuple(map(flat, (rate_one, bias_one, skip_one, rate_two, bias_two, skip_two)))
+    small += (out_w, flat(norm_gain), flat(pre_gain), in_w, step_w.T, conv_w)
+    small += (flat(conv_bias), flat(final_gain))
+    block = pltpu.VMEM((rows, slab), BF)
+    blocks = pltpu.VMEM((peers, rows, slab), BF)
+    tiles = pltpu.VMEM((peers, 8, rows), F32)
+    sends = pltpu.SemaphoreType.DMA((KINDS, peers))
     return pl.pallas_call(
         functools.partial(fused, peers, heads),
         out_shape=jax.ShapeDtypeStruct((tok_rows, inner_width), BF),
-        in_specs=specs,
-        out_specs=vmem,
-        scratch_shapes=[
-            pltpu.VMEM(out_w.shape, BF),
-            pltpu.VMEM(in_w.shape, BF),
-            pltpu.VMEM((rows, slab), BF),
-            pltpu.VMEM((rows, slab), BF),
+        in_specs=[pl.BlockSpec(memory_space=pltpu.HBM)] * (len(big) + len(small)),
+        out_specs=pl.BlockSpec(memory_space=pltpu.VMEM),
+        scratch_shapes=[pltpu.VMEM(part.shape, part.dtype) for part in small]
+        + [
+            block,
+            block,
             pltpu.VMEM((rows, state2), BF),
             pltpu.VMEM((rows, raw.shape[1]), F32),
-            pltpu.VMEM((rows, slab), BF),
-            pltpu.VMEM((peers, rows, slab), BF),
-            pltpu.VMEM((peers, rows, slab), BF),
+            block,
+            blocks,
+            blocks,
             pltpu.VMEM((8, rows), F32),
-            pltpu.VMEM((peers, 8, rows), F32),
-            pltpu.VMEM((peers, rows, slab), BF),
-            pltpu.VMEM((peers, rows, slab), BF),
+            tiles,
+            blocks,
+            blocks,
             pltpu.VMEM((rows, state2), BF),
-            pltpu.VMEM((peers, rows, state2), BF),
-            pltpu.VMEM((peers, 8, rows), F32),
-            pltpu.VMEM((peers, 8, rows), F32),
-            pltpu.VMEM((rows, slab), BF),
+            pltpu.VMEM((peers, tok_rows, state2), BF),
+            pltpu.VMEM((tok_rows, state2), BF),
+            pltpu.VMEM((rows, state2), BF),
+            tiles,
+            tiles,
+            block,
             pltpu.VMEM((tok_rows, inner_width), BF),
             pltpu.VMEM((rows, rows), F32),
-            pltpu.SemaphoreType.DMA((2,)),
-            pltpu.SemaphoreType.DMA((KINDS, peers)),
-            pltpu.SemaphoreType.DMA((KINDS, peers)),
+            pltpu.SemaphoreType.DMA((LOADS,)),
+            sends,
+            sends,
         ],
         compiler_params=pltpu.CompilerParams(
-            collective_id=0, has_side_effects=True, vmem_limit_bytes=40 * 1024 * 1024
+            collective_id=0, has_side_effects=True, vmem_limit_bytes=60 * 1024 * 1024
         ),
-    )(
-        inner,
-        gate,
-        bc,
-        raw,
-        flat(rate_one),
-        flat(bias_one),
-        flat(skip_one),
-        flat(norm_gain),
-        out_w,
-        residual,
-        flat(pre_gain),
-        in_w,
-        conv_w,
-        flat(conv_bias),
-        step_w,
-        flat(bias_two),
-        flat(rate_two),
-        flat(skip_two),
-        flat(final_gain),
-    )
+    )(*big, *small)
 
 
 def local_step(peers, *args):

time: 74.3 us -> 54.5 us (0.73)
  local copies, waits for them, and re-layouts: 15.7 us -> 2.78 us
  Pallas kernels: 57.8 us -> 51.5 us
    unnamed x36 -> x1, local copies, waits for them, and re-layouts: 14.9 us -> 1.47 us
    pallas_call x1, Pallas kernels: 57.8 us -> 51.5 us  [fused_local(): pl.pallas_call(functools.partial(fused, peers, heads), out_shape=jax.Shap...]
where the time goes in v2:
time: 54.5 us; the launch traced here: 54.3 us
  Pallas kernels  51.5 us (94%)
  local copies, waits for them, and re-layouts  2.78 us (5%)
    pallas_call x1, Pallas kernels, fused_local(): pl.pallas_call(functools.partial(fused, peers, heads), out_shape=jax.Shap...  51.5 us
    unnamed x1, local copies, waits for them, and re-layouts  1.47 us
    reshape x1, local copies, waits for them, and re-layouts, flat(): return vector.reshape(1, vector.shape[0])  1.31 us

profile of v2, /device:TPU:0, one launch (start us, length us, event | category | flops | bytes accessed | tf_op | source)
XLA Modules:
  0.0 54.3 jit_solution(1333443527428287406)
XLA Ops:
  0.0 1.3 %reshape.38.refs_17_ = f32[1,2304]{1,0:T(1,128)} reshape(f32[2304]{0:T(1024)} %param.32) | data formatting | bytes 18432 | tf_op jit(solution)/shard_map/reshape | solution.py:479
  1.3 51.5 %shard_map.181 = bf16[16,2048]{1,0:T(8,128)(2,1)} custom-call(bf16[16,2048]{1,0:T(8,128)(2,1)} %refs_0_.1, bf16[16,2048]{1,0:T(8,128)(2,1)} %refs_1_.1, bf16[16,256]{1,0:T(8,128)(2,1)} %refs_2_.1, f32[16,32]{1,0:T(8,128)} %refs_3_.1, bf16[16,2048]{1,0:T(8,128)(2,1)} %refs_4_.1, f32[1,32]{1,0:T(1,128)} %bitcast.14, f32[1,32]{1,0:T(1,128)} %bitcast.15, ...), custom_call_target="tpu_custom_call" | custom-call | tf_op jit(solution)/shard_map/pallas_call | solution.py:489
  52.8 1.5 %copy.21 = bf16[16,2048]{1,0:T(8,128)(2,1)} copy(bf16[16,2048]{1,0:T(8,128)(2,1)} %shard_map.181) | data formatting | bytes 131072

commit v3 on v2

--- a/solution.py
+++ b/solution.py
@@ -272,13 +272,18 @@
 
     flights = []
 
-    def send(kind, d, src, dst):
+    chips, core = (peers // 2, lax.rem(me, 2))
+    chip = lax.div(me, 2)
+    partner = me + 1 - 2 * core
+    hops = sorted(range(1, chips), key=lambda k: -min(k, chips - k))
+
+    def send(kind, d, src, dst, target=None):
         copy = pltpu.make_async_remote_copy(
             src_ref=src,
             dst_ref=dst,
             send_sem=send_sem.at[kind, d],
             recv_sem=recv_sem.at[kind, d],
-            device_id={"tok": peer(d)},
+            device_id={"tok": peer(d) if target is None else target},
             device_id_type=MESH,
         )
         copy.start()
@@ -318,6 +323,37 @@
         first[GATE_K, d] = send(GATE_K, d, gate.at[:, at(peer(d), slab)], gate_all.at[my_rows, :])
     for d in order:
         first[RES_K, d] = send(RES_K, d, residual.at[:, at(peer(d), slab)], res_all.at[my_rows, :])
+
+    def exchange(kind, left, weights, tx, rx):
+        def device(k, side):
+            return 2 * lax.rem(chip + k, chips) + side
+
+        def partial(index):
+            return jnp.dot(left, weights[:, at(index, slab)], preferred_element_type=F32)
+
+        halves, crossed = ({}, {})
+        for k in hops + [0]:
+            tx[k] = partial(device(k, 1 - core)).astype(BF)
+            halves[k] = send(kind, k, tx.at[k], rx.at[k], partner)
+
+        def joined(k):
+            own = partial(device(k, core))
+            halves[k].wait_recv()
+            return own + rx[k].astype(F32)
+
+        def forward(k):
+            slot = chips + k
+            tx[slot] = joined(k).astype(BF)
+            crossed[slot] = send(kind, slot, tx.at[slot], rx.at[slot], device(k, core))
+
+        def total():
+            value = joined(0)
+            for slot, copy in crossed.items():
+                copy.wait_recv()
+                value = value + rx[slot].astype(F32)
+            return value
+
+        return forward, total
 
     def arrived(copies, *kinds):
         for kind in kinds:
@@ -360,12 +396,9 @@
     loads[11].wait()
     loads[12].wait()
     scaled = (gated * norm_gain[:, mine]).astype(BF)
-    for d in order:
-        out_tx[d] = jnp.dot(
-            scaled, out_w[:, at(peer(d), slab)], preferred_element_type=F32
-        ).astype(BF)
-        second[OUT_K, d] = send(OUT_K, d, out_tx.at[d], out_rx.at[d])
-    hidden = jnp.dot(scaled, out_w[:, mine], preferred_element_type=F32)
+    forward, total = exchange(OUT_K, scaled, out_w, out_tx, out_rx)
+    for k in hops:
+        forward(k)
     loads[4].wait()
     arrived(first, RES_K)
     arrived(second, SQ1_K)
@@ -373,10 +406,7 @@
     for d in order:
         squares = squares + sq1_rx[d]
     scale = as_column(lax.rsqrt(squares[0:1] / inner_width + 1e-05))
-    for d in order:
-        second[OUT_K, d].wait_recv()
-        hidden = hidden + out_rx[d].astype(F32)
-    hidden = (res_all[...].astype(F32) + scale * hidden).astype(BF)
+    hidden = (res_all[...].astype(F32) + scale * total()).astype(BF)
     to = lax.broadcasted_iota(jnp.int32, (rows, rows), 0)
     raster = lax.broadcasted_iota(jnp.int32, (rows, rows), 1)
     moved = (raster % peers) * (rows // peers) + raster // peers
@@ -404,12 +434,9 @@
             PROJ_K, d, proj_tx.at[at(peer(d), tok_rows), :], proj_rx.at[d]
         )
 
-    def send_values(d):
-        val_tx[d] = jnp.dot(pre, in_w[:, at(peer(d), slab)], preferred_element_type=F32).astype(BF)
-        third[VAL_K, d] = send(VAL_K, d, val_tx.at[d], val_rx.at[d])
-
-    for d in order[0:4]:
-        send_values(d)
+    forward, total = exchange(VAL_K, pre, in_w, val_tx, val_rx)
+    for k in hops[:1]:
+        forward(k)
     proj = proj_tx[my_rows, :].astype(F32)
     for d in order:
         third[PROJ_K, d].wait_recv()
@@ -418,9 +445,8 @@
     for d in order:
         third[SPREAD_K, d] = send(SPREAD_K, d, spread_tx, proj_all.at[my_rows, :])
     proj_all[my_rows, :] = spread_tx[...]
-    for d in order[4:]:
-        send_values(d)
-    value = jnp.dot(pre, in_w[:, mine], preferred_element_type=F32)
+    for k in hops[1:]:
+        forward(k)
     arrived(third, SQ2_K)
     gathered = sq2_tx[me]
     for d in order:
@@ -432,22 +458,19 @@
     def convolve(projected, columns):
         taps = conv_weight[:, columns].astype(F32)
         place = lax.broadcasted_iota(jnp.int32, projected.shape, 0)
-        total = conv_bias[:, columns]
+        mixed = conv_bias[:, columns]
         for offset in range(KC):
             back = KC - 1 - offset
             term = projected
             if back:
                 term = jnp.where(place < back, 0.0, pltpu.roll(projected, back, 0))
-            total = total + taps[offset : offset + 1] * term
-        return jax.nn.silu(total).astype(BF)
+            mixed = mixed + taps[offset : offset + 1] * term
+        return jax.nn.silu(mixed).astype(BF)
 
     arrived(third, SPREAD_K)
     both = convolve(scale * proj_all[...].astype(F32), slice(inner_width, width))
-    for d in order:
-        third[VAL_K, d].wait_recv()
-        value = value + val_rx[d].astype(F32)
     scanned = ssd_heads(
-        convolve(scale * value, mine),
+        convolve(scale * total(), mine),
         both[:, 0:state],
         both[:, state : 2 * state],
         steps,
@@ -529,6 +552,7 @@
     heads = rates.shape[0]
     fits = (
         tok_rows * peers == 128
+        and peers % 2 == 0
         and tok_rows % 16 == 0
         and tok_rows % peers == 0
         and heads % peers == 0

time: 54.5 us -> 44.5 us (0.82)
  Pallas kernels: 51.5 us -> 41.5 us
    pallas_call x1, Pallas kernels: 51.5 us -> 41.5 us  [fused_local(): pl.pallas_call(functools.partial(fused, peers, heads), out_shape=jax.Shap...]
where the time goes in v3:
time: 44.5 us; the launch traced here: 44.3 us
  Pallas kernels  41.5 us (93%)
  local copies, waits for them, and re-layouts  2.78 us (6%)
    pallas_call x1, Pallas kernels, fused_local(): pl.pallas_call(functools.partial(fused, peers, heads), out_shape=jax.Shap...  41.5 us
    unnamed x1, local copies, waits for them, and re-layouts  1.47 us
    reshape x1, local copies, waits for them, and re-layouts, flat(): return vector.reshape(1, vector.shape[0])  1.31 us

profile of v3, /device:TPU:0, one launch (start us, length us, event | category | flops | bytes accessed | tf_op | source)
XLA Modules:
  0.0 44.3 jit_solution(9386282767189957392)
XLA Ops:
  0.0 1.3 %reshape.38.refs_17_ = f32[1,2304]{1,0:T(1,128)} reshape(f32[2304]{0:T(1024)} %param.32) | data formatting | bytes 18432 | tf_op jit(solution)/shard_map/reshape | solution.py:502
  1.3 41.5 %shard_map.181 = bf16[16,2048]{1,0:T(8,128)(2,1)} custom-call(bf16[16,2048]{1,0:T(8,128)(2,1)} %refs_0_.1, bf16[16,2048]{1,0:T(8,128)(2,1)} %refs_1_.1, bf16[16,256]{1,0:T(8,128)(2,1)} %refs_2_.1, f32[16,32]{1,0:T(8,128)} %refs_3_.1, bf16[16,2048]{1,0:T(8,128)(2,1)} %refs_4_.1, f32[1,32]{1,0:T(1,128)} %bitcast.14, f32[1,32]{1,0:T(1,128)} %bitcast.15, ...), custom_call_target="tpu_custom_call" | custom-call | tf_op jit(solution)/shard_map/pallas_call | solution.py:512
  42.8 1.5 %copy.21 = bf16[16,2048]{1,0:T(8,128)(2,1)} copy(bf16[16,2048]{1,0:T(8,128)(2,1)} %shard_map.181) | data formatting | bytes 131072

commit v4 on v3

--- a/solution.py
+++ b/solution.py
@@ -216,9 +216,8 @@
     return jnp.broadcast_to(column, (rows, rows)).T[0:8]
 
 
-def ssd_heads(values, write_side, read_side, steps, rates, skips, heads, tmp):
-    rows, width = values.shape
-    head = width // heads
+def mixweights(write_side, read_side, steps, rates, heads, tmp):
+    rows = write_side.shape[0]
     at = lax.broadcasted_iota(jnp.int32, (rows, rows), 0)
     source = lax.broadcasted_iota(jnp.int32, (rows, rows), 1)
     ahead = (at <= source).astype(F32)
@@ -236,7 +235,13 @@
         gap = columns[:, h : h + 1] - cumulative[h : h + 1, :]
         decay = jnp.exp(jnp.where(lower, gap, -1e30))
         mixing.append((scores * decay * steps[h : h + 1, :]).astype(BF))
-    product = jnp.dot(jnp.concatenate(mixing, axis=0), values, preferred_element_type=F32)
+    return jnp.concatenate(mixing, axis=0)
+
+
+def apply_mix(mixing, values, skips, heads):
+    rows, width = values.shape
+    head = width // heads
+    product = jnp.dot(mixing, values, preferred_element_type=F32)
     owner = lax.broadcasted_iota(jnp.int32, (rows, width), 1) // head
     wide = values.astype(F32)
     result = jnp.zeros((rows, width), F32)
@@ -253,7 +258,7 @@
     (out_w, norm_gain, pre_gain, in_w, step_weight, conv_weight, conv_bias, final_gain) = small[6:14]
     (inner_all, gate_all, bc_all, raw_all, res_all, out_tx, out_rx, sq1_tx, sq1_rx) = refs[34:43]
     (val_tx, val_rx, proj_tx, proj_rx, spread_tx, proj_all, sq2_tx, sq2_rx) = refs[43:51]
-    (fin_tx, fin, tmp, load_sem, send_sem, recv_sem) = refs[51:57]
+    (fin_tx, fin, tmp, mixing_ref, load_sem, send_sem, recv_sem) = refs[51:58]
     tok_rows, inner_width = inner.shape
     rows = tok_rows * peers
     slab = inner_width // peers
@@ -374,18 +379,13 @@
     tmp[:, 0:total_heads] = raw_all[...]
     steps = softplus(pltpu.roll(tmp[...], turn, 1).T[0:8] + params[0:8, 1:2])
     loads[1].wait()
+    arrived(first, BC_K)
+    mixing_ref[...] = mixweights(
+        bc_all[:, 0:state], bc_all[:, state : 2 * state], steps, params[0:8, 0:1], heads, tmp
+    )
     loads[2].wait()
-    arrived(first, BC_K, INNER_K)
-    scanned = ssd_heads(
-        inner_all[...],
-        bc_all[:, 0:state],
-        bc_all[:, state : 2 * state],
-        steps,
-        params[0:8, 0:1],
-        params[0:8, 2:3],
-        heads,
-        tmp,
-    )
+    arrived(first, INNER_K)
+    scanned = apply_mix(mixing_ref[...], inner_all[...], params[0:8, 2:3], heads)
     loads[3].wait()
     arrived(first, GATE_K)
     gated = scanned * jax.nn.silu(gate_all[...].astype(F32))
@@ -455,10 +455,14 @@
     scale = as_column(scale_row)
     steps = softplus(scale_row * gathered + params[0:8, 4:5])
 
-    def convolve(projected, columns):
+    def bias_row(start, size):
+        pieces = [conv_bias[pl.ds(start + i, 1), :] for i in range(size // 128)]
+        return jnp.concatenate(pieces, axis=1)
+
+    def convolve(projected, columns, bias):
         taps = conv_weight[:, columns].astype(F32)
         place = lax.broadcasted_iota(jnp.int32, projected.shape, 0)
-        mixed = conv_bias[:, columns]
+        mixed = bias
         for offset in range(KC):
             back = KC - 1 - offset
             term = projected
@@ -468,17 +472,12 @@
         return jax.nn.silu(mixed).astype(BF)
 
     arrived(third, SPREAD_K)
-    both = convolve(scale * proj_all[...].astype(F32), slice(inner_width, width))
-    scanned = ssd_heads(
-        convolve(scale * total(), mine),
-        both[:, 0:state],
-        both[:, state : 2 * state],
-        steps,
-        params[0:8, 3:4],
-        params[0:8, 5:6],
-        heads,
-        tmp,
-    ).astype(BF)
+    both = convolve(scale * proj_all[...].astype(F32), slice(inner_width, width), bias_row(inner_width // 128, width - inner_width))
+    mixing_ref[...] = mixweights(
+        both[:, 0:state], both[:, state : 2 * state], steps, params[0:8, 3:4], heads, tmp
+    )
+    values = convolve(scale * total(), mine, bias_row(me * (slab // 128), slab))
+    scanned = apply_mix(mixing_ref[...], values, params[0:8, 5:6], heads).astype(BF)
     fin_tx[...] = scanned
     last = {}
     for d in order:
@@ -504,7 +503,7 @@
     big = (inner, gate, bc, raw, residual)
     small = tuple(map(flat, (rate_one, bias_one, skip_one, rate_two, bias_two, skip_two)))
     small += (out_w, flat(norm_gain), flat(pre_gain), in_w, step_w.T, conv_w)
-    small += (flat(conv_bias), flat(final_gain))
+    small += (conv_bias.reshape(-1, 128), flat(final_gain))
     block = pltpu.VMEM((rows, slab), BF)
     blocks = pltpu.VMEM((peers, rows, slab), BF)
     tiles = pltpu.VMEM((peers, 8, rows), F32)
@@ -536,6 +535,7 @@
             block,
             pltpu.VMEM((tok_rows, inner_width), BF),
             pltpu.VMEM((rows, rows), F32),
+            pltpu.VMEM((heads * rows, rows), BF),
             pltpu.SemaphoreType.DMA((LOADS,)),
             sends,
             sends,

time: 44.5 us -> 42.8 us (0.962)
  local copies, waits for them, and re-layouts: 2.78 us -> 1.47 us
    reshape x1 -> x0, local copies, waits for them, and re-layouts: 1.31 us -> none  [flat(): return vector.reshape(1, vector.shape[0])]
where the time goes in v4:
time: 42.8 us; the launch traced here: 42.6 us
  Pallas kernels  41.1 us (96%)
  local copies, waits for them, and re-layouts  1.47 us (3%)
    pallas_call x1, Pallas kernels, fused_local(): pl.pallas_call(functools.partial(fused, peers, heads), out_shape=jax.Shap...  41.1 us
    unnamed x1, local copies, waits for them, and re-layouts  1.47 us

profile of v4, /device:TPU:0, one launch (start us, length us, event | category | flops | bytes accessed | tf_op | source)
XLA Modules:
  0.0 42.6 jit_solution(369464204624329771)
XLA Ops:
  0.0 41.1 %shard_map.181 = bf16[16,2048]{1,0:T(8,128)(2,1)} custom-call(bf16[16,2048]{1,0:T(8,128)(2,1)} %refs_0_.1, bf16[16,2048]{1,0:T(8,128)(2,1)} %refs_1_.1, bf16[16,256]{1,0:T(8,128)(2,1)} %refs_2_.1, f32[16,32]{1,0:T(8,128)} %refs_3_.1, bf16[16,2048]{1,0:T(8,128)(2,1)} %refs_4_.1, f32[1,32]{1,0:T(1,128)} %bitcast.16, f32[1,32]{1,0:T(1,128)} %bitcast.17, ...), custom_call_target="tpu_custom_call" | custom-call | tf_op jit(solution)/shard_map/pallas_call | solution.py:511
  41.1 1.5 %copy.21 = bf16[16,2048]{1,0:T(8,128)(2,1)} copy(bf16[16,2048]{1,0:T(8,128)(2,1)} %shard_map.181) | data formatting | bytes 131072

commit v5 on v4

--- a/solution.py
+++ b/solution.py
@@ -321,6 +321,7 @@
     for d in order:
         first[RAW_K, d] = send(RAW_K, d, raw, raw_all.at[my_rows, :])
         first[BC_K, d] = send(BC_K, d, bc, bc_all.at[my_rows, :])
+    for d in order:
         first[INNER_K, d] = send(
             INNER_K, d, inner.at[:, at(peer(d), slab)], inner_all.at[my_rows, :]
         )

time: 42.8 us -> 42.8 us (level)
  no operation moved by 1% of the time
where the time goes in v5:
time: 42.8 us; the launch traced here: 42.6 us
  Pallas kernels  41.1 us (96%)
  local copies, waits for them, and re-layouts  1.47 us (3%)
    pallas_call x1, Pallas kernels, fused_local(): pl.pallas_call(functools.partial(fused, peers, heads), out_shape=jax.Shap...  41.1 us
    unnamed x1, local copies, waits for them, and re-layouts  1.47 us

profile of v5, /device:TPU:0, one launch (start us, length us, event | category | flops | bytes accessed | tf_op | source)
XLA Modules:
  0.0 42.6 jit_solution(15310404822579820572)
XLA Ops:
  0.0 41.1 %shard_map.181 = bf16[16,2048]{1,0:T(8,128)(2,1)} custom-call(bf16[16,2048]{1,0:T(8,128)(2,1)} %refs_0_.1, bf16[16,2048]{1,0:T(8,128)(2,1)} %refs_1_.1, bf16[16,256]{1,0:T(8,128)(2,1)} %refs_2_.1, f32[16,32]{1,0:T(8,128)} %refs_3_.1, bf16[16,2048]{1,0:T(8,128)(2,1)} %refs_4_.1, f32[1,32]{1,0:T(1,128)} %bitcast.16, f32[1,32]{1,0:T(1,128)} %bitcast.17, ...), custom_call_target="tpu_custom_call" | custom-call | tf_op jit(solution)/shard_map/pallas_call | solution.py:512
  41.1 1.5 %copy.21 = bf16[16,2048]{1,0:T(8,128)(2,1)} copy(bf16[16,2048]{1,0:T(8,128)(2,1)} %shard_map.181) | data formatting | bytes 131072
